TPU v7x, 256 devices: a whole 4x4x8 slice. The times are simulated.
256 devices in a mesh: row: 16 (over y_hi, z), col: 16 (over y_lo, x, core).
Axes of the slice: x: 4, y: 4 (y_hi: 2, y_lo: 2; y = y_hi * 2 + y_lo), z: 8, core: 2. Of those that a mesh axis runs over, the one named last changes fastest.
Arguments:
- design: bfloat16 [256, 24576], P('row', 'col'), may hold values from -0.375 to 0.375
- filter_taps: float32 [256], replicated, may hold values from -0.21875 to 0.21875
- probes: float32 [24576, 128], P('row', 'col'), may hold values from -576 to 576
- lower_bound: float32 [1], replicated, may hold values from 6 to 24
- upper_bound: float32 [1], replicated, may hold values from 192 to 288
Outputs:
- normal: float32 [24576, 24576], P('row', 'col')
- solution: float32 [24576, 128], P('row', 'col')
All inputs are finite; a program needn't handle non-finite values.
Results may differ from a plain program's by a relative error of at most 0.0072.
The roundings to bfloat16 on the way count: a program that leaves them out, or rounds other values in their place, can miss the bound.
Values may be sent and summed in bfloat16 or wider, within the bound.
A program may use at most 64 MiB of HBM per device.

v0:
```python
import jax
import jax.numpy as jnp
from jax import lax
from jax.sharding import PartitionSpec as P

SWEEPS = 2


def broadcast(block, axis, owner):
    block = jnp.where(lax.axis_index(axis) == owner, block, jnp.zeros_like(block))
    return lax.psum(block, axis)


def whitening(filter_taps):
    count = filter_taps.shape[0]
    padded = jnp.concatenate([filter_taps, jnp.zeros_like(filter_taps)])
    repeated = jnp.tile(padded, count)[: count * (2 * count - 1)]
    upper = repeated.reshape(count, 2 * count - 1)[:, :count]
    matrix = upper.T + jnp.eye(count, dtype=filter_taps.dtype)
    return matrix.astype(jnp.bfloat16)


def tile_product(normal_tile, direction_full, fetch):
    piece = fetch(direction_full, 0)
    partial_sum = jnp.dot(normal_tile, piece, precision=lax.Precision.HIGHEST)
    return partial_sum


def body(design, filter_taps, probes, lower_bound, upper_bound):
    row_count = lax.axis_size("row")
    col_count = lax.axis_size("col")
    fold_ratio = row_count // col_count
    row_index = lax.axis_index("row")
    col_index = lax.axis_index("col")
    filter_matrix = whitening(filter_taps)
    whole_panel = lax.all_gather(design, "row", axis=0, tiled=True)
    white = jnp.dot(filter_matrix, whole_panel, preferred_element_type=jnp.float32).astype(
        jnp.bfloat16
    )
    panel = broadcast(white, "col", row_index // fold_ratio)
    normal_tile = lax.dot_general(
        panel, white, (((0,), (0,)), ((), ())), preferred_element_type=jnp.float32
    )
    panel_wide = panel.astype(jnp.float32)
    jacobi = (jnp.sum(jnp.square(panel_wide), axis=0) + 1e-06)[:, None]
    center_value = (lower_bound[0] + upper_bound[0]) / 2.0
    half_width = (upper_bound[0] - lower_bound[0]) / 2.0
    sigma_value = center_value / half_width
    weight_now = 1.0 / sigma_value

    def fetch_whole(direction_full, block_index):
        return broadcast(
            direction_full.astype(jnp.bfloat16), "row", col_index * fold_ratio + block_index
        ).astype(direction_full.dtype)

    residual = lax.all_gather(probes, "col", axis=1, tiled=True)
    direction = residual / jacobi / center_value
    solution = jnp.zeros_like(residual)
    for sweep_index in range(SWEEPS):
        solution = solution + direction
        partial_sum = tile_product(normal_tile, direction, fetch_whole)
        residual = residual - lax.psum(partial_sum.astype(jnp.bfloat16), "col").astype(jnp.float32)
        weight_next = 1.0 / (2.0 * sigma_value - weight_now)
        direction = weight_next * weight_now * direction + 2.0 * weight_next / half_width * (
            residual / jacobi
        )
        weight_now = weight_next
    solution = solution + direction
    solution = lax.dynamic_slice_in_dim(solution, col_index * probes.shape[1], probes.shape[1], 1)
    return (normal_tile, solution)


def solution(mesh):
    placed = (P("row", "col"), P(), P("row", "col"), P(), P())
    return jax.shard_map(
        body,
        mesh=mesh,
        in_specs=placed,
        out_specs=(P("row", "col"), P("row", "col")),
        check_vma=False,
    )
```

profile of v0, /device:TPU:1, one launch (start us, length us, event | category | flops | bytes accessed | tf_op | source)
XLA Modules:
  0.0 761.7 jit_solution(446466744305148952)
XLA Ops:
  7.2 42.2 %all_gather.6 = bf16[256,1536]{1,0:T(8,128)(2,1)S(1)} all-gather(bf16[16,1536]{1,0:T(8,128)(2,1)} %param.5), channel_id=1, replica_groups=mesh['row'=16,'col'=16] {'row'}, dimensions={0}, use_global_device_ids=true | all-gather | bytes 835584 | tf_op jit(solution)/shard_map/all_gather | solution.py:36
  49.4 0.7 concatenate.3
  50.1 0.1 broadcast_bitcast_fusion
  50.1 0.1 copy.15
  50.3 0.4 reshape.17
  50.7 1.3 broadcast_select_fusion
  52.0 0.0 all-reduce.9.cloned.1.call-start
  52.1 29.6 %all_gather.7 = f32[1536,128]{0,1:T(8,128)S(1)} all-gather(f32[1536,8]{0,1:T(8,128)} %param.7), channel_id=1, replica_groups=mesh['row'=16,'col'=16] {'col'}, dimensions={1}, use_global_device_ids=true | all-gather | bytes 835584 | tf_op jit(solution)/shard_map/all_gather | solution.py:56
  81.7 0.3 copy.10
  83.3 94.2 %all-reduce.7.cloned.1.call-done = bf16[256,1536]{1,0:T(8,128)(2,1)} async-done(((bf16[256,1536]{1,0:T(8,128)(2,1)}), bf16[256,1536]{1,0:T(8,128)(2,1)}) %all-reduce.7.cloned.1.call-update) | async-done | bytes 786448 | tf_op jit(solution)/shard_map/psum | solution.py:11
  177.4 1.3 multiply_reduce_fusion
  178.7 1.0 convert_select_fusion.1
  179.8 0.0 all-reduce.11.cloned.1.call-start
  179.9 6.3 fusion.7
  186.2 141.6 %all-reduce.9.cloned.1.call-done = bf16[1536,128]{1,0:T(8,128)(2,1)} async-done(((bf16[1536,128]{1,0:T(8,128)(2,1)}), bf16[1536,128]{1,0:T(8,128)(2,1)}) %all-reduce.9.cloned.1.call-update) | async-done | bytes 393232 | tf_op jit(solution)/shard_map/psum | solution.py:11
  327.7 7.7 %convolution_convert_fusion.2 = bf16[1536,128]{1,0:T(8,128)(2,1)} fusion(f32[1536,1536]{1,0:T(8,128)} %fusion.7, bf16[1536,128]{1,0:T(8,128)(2,1)} %all-reduce.9.cloned.1.call-done), kind=kOutput, calls=%fused_computation.2 | convolution fusion | flops 3624075264 | bytes 10223616 | tf_op jit(solution)/shard_map/dot_general | solution.py:25
  335.7 129.3 %all-reduce.11.cloned.1.call-done = bf16[1536,128]{1,0:T(8,128)(2,1)} async-done(((bf16[1536,128]{1,0:T(8,128)(2,1)}), bf16[1536,128]{1,0:T(8,128)(2,1)}) %all-reduce.11.cloned.1.call-update) | async-done | bytes 393232 | tf_op jit(solution)/shard_map/psum | solution.py:62
  465.0 2.0 convert_select_fusion
  467.0 0.0 all-reduce.15.cloned.1.call-start
  467.1 148.0 %all-reduce.13.cloned.1.call-done = bf16[1536,128]{1,0:T(8,128)(2,1)} async-done(((bf16[1536,128]{1,0:T(8,128)(2,1)}), bf16[1536,128]{1,0:T(8,128)(2,1)}) %all-reduce.13.cloned.1.call-update) | async-done | bytes 393232 | tf_op jit(solution)/shard_map/psum | solution.py:11
  615.1 7.7 %convolution_convert_fusion.1 = bf16[1536,128]{1,0:T(8,128)(2,1)} fusion(f32[1536,1536]{1,0:T(8,128)} %fusion.7, bf16[1536,128]{1,0:T(8,128)(2,1)} %all-reduce.13.cloned.1.call-done), kind=kOutput, calls=%fused_computation.1 | convolution fusion | flops 3624075264 | bytes 10223616 | tf_op jit(solution)/shard_map/dot_general | solution.py:25
  622.9 129.5 %all-reduce.15.cloned.1.call-done = bf16[1536,128]{1,0:T(8,128)(2,1)} async-done(((bf16[1536,128]{1,0:T(8,128)(2,1)}), bf16[1536,128]{1,0:T(8,128)(2,1)}) %all-reduce.15.cloned.1.call-update) | async-done | bytes 393232 | tf_op jit(solution)/shard_map/psum | solution.py:62
  752.4 2.0 fusion
  754.4 0.9 copy.13
  (8 shorter events, 0.2 us)
Async XLA Ops:
  7.2 170.3 %all-reduce.7.cloned.1.call-start = ((), (), s32[]{:S(2)}) async-start(), calls=%async_computation | async-start | bytes 1572864 | tf_op jit(solution)/shard_map/psum | solution.py:11
  52.0 275.8 %all-reduce.9.cloned.1.call-start = ((), (), s32[]{:S(2)}) async-start(), calls=%async_computation.1 | async-start | bytes 786432 | tf_op jit(solution)/shard_map/psum | solution.py:11
  179.8 285.2 %all-reduce.11.cloned.1.call-start = ((), (), s32[]{:S(2)}) async-start(), calls=%async_computation.2 | async-start | bytes 786432 | tf_op jit(solution)/shard_map/psum | solution.py:62
  335.4 279.7 %all-reduce.13.cloned.1.call-start = ((), (), s32[]{:S(2)}) async-start(), calls=%async_computation.3 | async-start | bytes 786432 | tf_op jit(solution)/shard_map/psum | solution.py:11
  467.0 285.3 %all-reduce.15.cloned.1.call-start = ((), (), s32[]{:S(2)}) async-start(), calls=%async_computation.4 | async-start | bytes 786432 | tf_op jit(solution)/shard_map/psum | solution.py:62
Sparse Core Ops, SparseCore 0:
  52.1 125.2 all-reduce.6
  180.2 147.4 all-reduce.8
  335.6 129.3 all-reduce.10
  467.6 147.4 all-reduce.12
  622.9 129.3 all-reduce.14
where the time goes:
time: 762 us
  waiting for transfers between devices  643 us (84%)
  blocking collectives  71.8 us (9%)
  matrix products  22.9 us (3%)
  between operations  15.4 us (2%)
    psum x3, waiting for transfers between devices, broadcast(): return lax.psum(block, axis)  384 us
    psum x2, waiting for transfers between devices, body(): lax.psum(partial_sum.astype(jnp.bfloat16), 'col').astype(jnp.float32)  259 us
    all_gather x1, blocking collectives, body(): whole_panel = lax.all_gather(design, 'row', axis=0, tiled=True)  42.2 us
    all_gather x1, blocking collectives, body(): residual = lax.all_gather(probes, 'col', axis=1, tiled=True)  29.6 us
    dot_general x2, matrix products, tile_product(): partial_sum = jnp.dot(normal_tile, piece, precision=lax.Precision.HIGHEST)  15.4 us
  transfers between devices with their start and end apart: 5, of which 5 were waited for; matrix products, arithmetic and copies ran while one was open for 1% of the time, Pallas kernels for 0%

commit v1 on v0

v1 whole, which is shorter than its diff:
```python
import jax
import jax.numpy as jnp
from jax import lax
from jax.experimental import pallas as pl
from jax.experimental.pallas import tpu as pltpu
from jax.sharding import PartitionSpec as P

MESH = pl.DeviceIdType.MESH
F32 = jnp.float32
BF16 = jnp.bfloat16
EPOCHS = 256
SIDE = 16
BLOCK = 16
WIDTH = 1536
LANES = 128
CHUNKS = WIDTH // LANES


def owner_of(chunk):
    return (chunk // 3) * 4 + chunk % 3


def remote(src, dst, send, recv, device):
    return pltpu.make_async_remote_copy(
        src_ref=src, dst_ref=dst, send_sem=send, recv_sem=recv, device_id=device, device_id_type=MESH
    )


def split(value):
    high = value.astype(BF16)
    low = (value - high.astype(F32)).astype(BF16)
    return jnp.concatenate([high, low], axis=0)


def kernel(
    design, taps, probes, lower, upper,
    tile, answer,
    cbuf, rsub, wr, wc, usend, ubuf,
    c_send, c_recv, s_send, s_recv, g_send, g_fwd, g_recv, u_send, u_recv,
):
    r, c = lax.axis_index("row"), lax.axis_index("col")
    h, z = r // 8, r % 8
    l, x, k = c // 8, (c // 2) % 4, c % 2
    sibling = (r, c + 1 - 2 * k)
    z_next, z_prev = (h * 8 + (z + 1) % 8, c), (h * 8 + (z + 7) % 8, c)
    partner = ((1 - h) * 8 + z, c)
    is_owner = c % 4 != 3
    mine = (c // 4) * 3 + c % 4
    on_diagonal = r == c

    barrier = pltpu.get_barrier_semaphore()
    for o in range(1, SIDE):
        pl.semaphore_signal(barrier, inc=1, device_id=((r + o) % SIDE, c), device_id_type=MESH)
    for dl in range(2):
        for dx in range(4):
            if dl or dx:
                to = (r, ((l + dl) % 2) * 8 + ((x + dx) % 4) * 2 + k)
                pl.semaphore_signal(barrier, inc=1, device_id=to, device_id_type=MESH)
    pl.semaphore_signal(barrier, inc=1, device_id=sibling, device_id_type=MESH)
    for o in range(1, SIDE):
        pl.semaphore_signal(barrier, inc=1, device_id=((r + o) % SIDE, r), device_id_type=MESH)

    @pl.when(jnp.logical_not(on_diagonal))
    def _():
        pl.semaphore_signal(barrier, inc=1, device_id=(r, r), device_id_type=MESH)

    pl.semaphore_wait(barrier, 15 + 8 + 15 + jnp.where(on_diagonal, 0, 1))

    def block_of(other, steps):
        return ((1 - h) if other else h) * 8 + (z + steps + 16) % 8

    sends = []

    def ship(slot, block, to, src=None):
        copy = remote(
            cbuf.at[block] if src is None else src, cbuf.at[block], c_send.at[slot], c_recv.at[block], to
        )
        copy.start()
        sends.append(copy)

    def await_block(block):
        remote(cbuf.at[block], cbuf.at[block], c_send.at[0], c_recv.at[block], z_next).wait_recv()

    ship(0, r, z_next, design)
    ship(1, r, z_prev, design)
    ship(2, r, partner, design)

    scatter = []
    for chunk in range(CHUNKS):
        owner = owner_of(chunk)
        copy = remote(
            design.at[:, pl.ds(chunk * LANES, LANES)], rsub.at[r], s_send.at[chunk], s_recv.at[r], (c, owner)
        )
        away = jnp.logical_not(jnp.logical_and(on_diagonal, c == owner))
        scatter.append((away, copy))

        @pl.when(away)
        def _():
            copy.start()

        @pl.when(jnp.logical_not(away))
        def _():
            rsub[r] = design[:, chunk * LANES : (chunk + 1) * LANES]

    cbuf[r] = design[...]

    shape = (EPOCHS, EPOCHS)
    row_id = lax.broadcasted_iota(jnp.int32, shape, 0)
    col_id = lax.broadcasted_iota(jnp.int32, shape, 1)
    moved = jnp.broadcast_to(taps[...], shape)
    for bit in range(8):
        moved = jnp.where((row_id >> bit) % 2 == 1, pltpu.roll(moved, 1 << bit, 1), moved)
    moved = jnp.where(col_id >= row_id, moved, 0.0) + jnp.where(col_id == row_id, 1.0, 0.0)
    filt = moved.T.astype(BF16)

    def whiten(raw):
        return jnp.dot(filt, raw, preferred_element_type=F32).astype(BF16)

    await_block(block_of(False, -1))
    ship(3, block_of(False, -1), z_next)
    await_block(block_of(False, 1))
    ship(4, block_of(False, 1), z_prev)
    await_block(block_of(True, 0))
    ship(5, block_of(True, 0), z_next)
    ship(6, block_of(True, 0), z_prev)

    gather = []

    @pl.when(is_owner)
    def _():
        for o in range(SIDE):
            source = (r + o) % SIDE

            def arrived():
                remote(rsub.at[source], rsub.at[source], s_send.at[0], s_recv.at[source], z_next).wait_recv()

            if o == 0:
                pl.when(jnp.logical_not(on_diagonal))(arrived)
            else:
                arrived()
        wr[mine] = whiten(rsub[...].reshape(EPOCHS, LANES))
        slot = 0
        for dl in range(2):
            for dx in range(4):
                to = sibling
                if dl or dx:
                    to = (r, ((l + dl) % 2) * 8 + ((x + dx) % 4) * 2 + k)
                copy = remote(wr.at[mine], wr.at[mine], g_send.at[slot], g_recv.at[mine], to)
                copy.start()
                gather.append(copy)
                slot += 1

    await_block(block_of(False, -2))
    ship(7, block_of(False, -2), z_next)
    await_block(block_of(False, 2))
    ship(8, block_of(False, 2), z_prev)
    await_block(block_of(True, -1))
    ship(9, block_of(True, -1), z_next)
    await_block(block_of(True, 1))
    ship(10, block_of(True, 1), z_prev)

    await_block(block_of(False, -3))
    await_block(block_of(False, 3))
    way = 1 - 2 * h
    own_way = (h * 8 + (z + way + 8) % 8, c)
    other_way = (h * 8 + (z - way + 8) % 8, c)
    ship(11, block_of(False, -3 * way), own_way)
    await_block(block_of(True, -2))
    ship(12, block_of(True, -2), z_next)
    await_block(block_of(True, 2))
    ship(13, block_of(True, 2), z_prev)

    forwards = []

    def chunk_arrived(chunk):
        remote(wr.at[chunk], wr.at[chunk], g_fwd.at[chunk], g_recv.at[chunk], sibling).wait_recv()

    for chunk in range(CHUNKS):
        owner = owner_of(chunk)
        relay = jnp.logical_and(c != owner, k == owner % 2)
        copy = remote(wr.at[chunk], wr.at[chunk], g_fwd.at[chunk], g_recv.at[chunk], sibling)
        forwards.append((relay, copy))

        @pl.when(relay)
        def _():
            chunk_arrived(chunk)
            copy.start()

    await_block(block_of(True, -3))
    await_block(block_of(True, 3))
    ship(14, block_of(True, 3 * way), other_way)

    for chunk in range(CHUNKS):
        owner = owner_of(chunk)

        @pl.when(k != owner % 2)
        def _():
            chunk_arrived(chunk)

    low = jnp.full((1, LANES), lower[0], F32)
    high = jnp.full((1, LANES), upper[0], F32)
    center = (low + high) / 2.0
    half = (high - low) / 2.0
    sigma = center / half
    rho0 = 1.0 / sigma
    rho1 = 1.0 / (2.0 * sigma - rho0)
    rho2 = 1.0 / (2.0 * sigma - rho1)

    last = (((1,), (1,)), ((), ()))

    def forward_product(parts):
        total = jnp.zeros((2 * 8, EPOCHS), F32)
        for chunk in range(CHUNKS):
            total += lax.dot_general(split(parts[chunk]), wr[chunk], last, preferred_element_type=F32)
        return total[:8] + total[8:]

    def back_product(whole, chunk):
        both = jnp.dot(whole, wr[chunk], preferred_element_type=F32)
        return both[:8] + both[8:]

    pending = []

    def exchange_start(turn, value):
        packed = jnp.concatenate([value[:, :LANES], value[:, LANES:]], axis=0).astype(BF16)
        usend[turn] = packed
        ubuf[turn, r] = packed
        for o in range(1, SIDE):
            copy = remote(
                usend.at[turn], ubuf.at[turn, r], u_send.at[turn, o], u_recv.at[turn, r], ((r + o) % SIDE, c)
            )
            copy.start()
            pending.append(copy)

    def exchange_finish(turn):
        for o in range(1, SIDE):
            source = (r + o) % SIDE
            slot = ubuf.at[turn, source]
            remote(slot, slot, u_send.at[turn, o], u_recv.at[turn, source], z_next).wait_recv()
        total = jnp.sum(ubuf[turn].astype(F32), axis=0)
        return jnp.concatenate([total[:8], total[8:]], axis=1)

    def rows_of(first, count):
        @pl.loop(first, first + count)
        def _(chunk):
            tile[pl.ds(pl.multiple_of(chunk * LANES, LANES), LANES), :] = lax.dot_general(
                wr[chunk], wc[...], (((0,), (0,)), ((), ())), preferred_element_type=F32
            )

    inverse, residual, direction = [], [], []
    for chunk in range(CHUNKS):
        wide = wr[chunk].astype(F32)
        jacobi = jnp.sum(wide * wide, axis=0, keepdims=True) + 1e-06
        right = probes[:, chunk * LANES : (chunk + 1) * LANES]
        inverse.append(1.0 / jacobi)
        residual.append(right)
        direction.append(right / jacobi / center)
    total = list(direction)
    exchange_start(0, forward_product(direction))

    await_block(block_of(False, 4))
    await_block(block_of(True, 4))
    wc[...] = whiten(cbuf[...].reshape(EPOCHS, WIDTH))
    rows_of(0, 6)

    product = split(exchange_finish(0))
    for chunk in range(CHUNKS):
        residual[chunk] = residual[chunk] - back_product(product, chunk)
        direction[chunk] = rho1 * rho0 * direction[chunk] + 2.0 * rho1 / half * (
            residual[chunk] * inverse[chunk]
        )
        total[chunk] = total[chunk] + direction[chunk]
    exchange_start(1, forward_product(direction))
    rows_of(6, 6)
    product = split(exchange_finish(1))
    for chunk in range(CHUNKS):
        residual[chunk] = residual[chunk] - back_product(product, chunk)
        direction[chunk] = rho2 * rho1 * direction[chunk] + 2.0 * rho2 / half * (
            residual[chunk] * inverse[chunk]
        )
        answer[:, chunk * LANES : (chunk + 1) * LANES] = total[chunk] + direction[chunk]

    for copy in sends + pending:
        copy.wait_send()
    for away, copy in scatter + forwards:
        pl.when(away)(copy.wait_send)

    @pl.when(is_owner)
    def _():
        for slot in range(8):
            remote(wr.at[mine], wr.at[mine], g_send.at[slot], g_recv.at[mine], sibling).wait_send()


def body(design, filter_taps, probes, lower_bound, upper_bound):
    vmem = pl.BlockSpec(memory_space=pltpu.VMEM)
    smem = pl.BlockSpec(memory_space=pltpu.SMEM)
    dma = pltpu.SemaphoreType.DMA
    tile, answer = pl.pallas_call(
        kernel,
        out_shape=(
            jax.ShapeDtypeStruct((WIDTH, WIDTH), F32),
            jax.ShapeDtypeStruct((8, WIDTH), F32),
        ),
        in_specs=[vmem, vmem, vmem, smem, smem],
        out_specs=(vmem, vmem),
        scratch_shapes=[
            pltpu.VMEM((SIDE, BLOCK, WIDTH), BF16),
            pltpu.VMEM((SIDE, BLOCK, LANES), BF16),
            pltpu.VMEM((CHUNKS, EPOCHS, LANES), BF16),
            pltpu.VMEM((EPOCHS, WIDTH), BF16),
            pltpu.VMEM((2, 16, LANES), BF16),
            pltpu.VMEM((2, SIDE, 16, LANES), BF16),
            dma((15,)), dma((SIDE,)),
            dma((CHUNKS,)), dma((SIDE,)),
            dma((8,)), dma((CHUNKS,)), dma((CHUNKS,)),
            dma((2, SIDE)), dma((2, SIDE)),
        ],
        compiler_params=pltpu.CompilerParams(
            collective_id=1, has_side_effects=True, vmem_limit_bytes=40 << 20
        ),
        name="gather_and_solve",
    )(design, filter_taps.reshape(1, EPOCHS), probes.T, lower_bound, upper_bound)
    return tile, answer.T


def solution(mesh):
    placed = (P("row", "col"), P(), P("row", "col"), P(), P())
    return jax.shard_map(
        body,
        mesh=mesh,
        in_specs=placed,
        out_specs=(P("row", "col"), P("row", "col")),
        check_vma=False,
    )
```

time: 762 us -> 51.9 us (0.07)
  waiting for transfers between devices: 643 us -> 0 us
  blocking collectives: 71.8 us -> 0 us
  Pallas kernels: 0 us -> 43.1 us
  matrix products: 22.9 us -> 0 us
  between operations: 15.4 us -> 1.94 us
    psum x5 -> x0, waiting for transfers between devices: 643 us -> none  [the longest x3 384 us: broadcast(): return lax.psum(block, axis)]
    all_gather x2 -> x0, blocking collectives: 71.8 us -> none  [the longest x1 42.2 us: body(): whole_panel = lax.all_gather(design, 'row', axis=0, tiled=True)]
    pallas_call x0 -> x1, Pallas kernels: none -> 43.1 us  [body(): pl.pallas_call(kernel, out_shape=(jax.ShapeDtypeStruct((WIDTH, WIDTH), F3...]
    dot_general x4 -> x0, matrix products: 22.9 us -> none  [the longest x2 15.4 us: tile_product(): partial_sum = jnp.dot(normal_tile, piece, precision=lax.Precision.HIGHEST)]
  transfers between devices with their start and end apart: 5 -> 0, of which waited for: 5 -> 0; matrix products, arithmetic and copies ran while one was open for 1% -> 0% of each run, Pallas kernels for 0% -> 0%
where the time goes in v1:
time: 51.9 us; the launch traced here: 51.7 us
  Pallas kernels  43.1 us (83%)
  local copies, waits for them, and re-layouts  6.63 us (13%)
  between operations  1.94 us (4%)
    pallas_call x1, Pallas kernels, body(): pl.pallas_call(kernel, out_shape=(jax.ShapeDtypeStruct((WIDTH, WIDTH), F3...  43.1 us
    unnamed x8, local copies, waits for them, and re-layouts  6.63 us

profile of v1, /device:TPU:1, one launch (start us, length us, event | category | flops | bytes accessed | tf_op | source)
XLA Modules:
  0.0 51.7 jit_solution(6895020784636906733)
XLA Ops:
  1.9 0.0 copy-start
  1.9 0.8 %copy-done = bf16[16,1536]{1,0:T(8,128)(2,1)S(1)} copy-done((bf16[16,1536]{1,0:T(8,128)(2,1)S(1)}, bf16[16,1536]{1,0:T(8,128)(2,1)}, u32[]{:S(2)}) %copy-start) | copy-done | bytes 49176
  2.7 0.0 copy-start.1
  2.7 0.8 %copy-done.1 = f32[1536,8]{0,1:T(8,128)S(1)} copy-done((f32[1536,8]{0,1:T(8,128)S(1)}, f32[1536,8]{0,1:T(8,128)}, u32[]{:S(2)}) %copy-start.1) | copy-done | bytes 49176
  3.5 0.0 copy-start.2
  3.5 0.7 %copy-done.2 = f32[256]{0:T(256)S(1)} copy-done((f32[256]{0:T(256)S(1)}, f32[256]{0:T(256)}, u32[]{:S(2)}) %copy-start.2) | copy-done | bytes 1048
  4.2 43.1 %gather_and_solve.1 = (f32[1536,1536]{1,0:T(8,128)S(1)}, f32[8,1536]{1,0:T(8,128)S(1)}) custom-call(bf16[16,1536]{1,0:T(8,128)(2,1)S(1)} %copy-done, f32[1,256]{1,0:T(1,128)S(1)} %bitcast.5, f32[8,1536]{1,0:T(8,128)S(1)} %bitcast.3, f32[1]{0:T(128)S(6)} %copy.9.lower, f32[1]{0:T(128)S(6)} %copy.10.upper), custom_call_target="tpu_custom_call" | custom-call | tf_op jit(solution)/shard_map/gather_and_solve/pallas_call | solution.py:297
  47.4 3.7 %copy.11 = f32[1536,1536]{1,0:T(8,128)} copy(f32[1536,1536]{1,0:T(8,128)S(1)} %get-tuple-element.8) | data formatting | bytes 18874368
  51.1 0.6 %copy.12 = f32[1536,8]{0,1:T(8,128)} copy(f32[1536,8]{0,1:T(8,128)S(1)} %bitcast.4) | data formatting | bytes 98304
Async XLA Ops:
  1.9 0.8 %copy-start = (bf16[16,1536]{1,0:T(8,128)(2,1)S(1)}, bf16[16,1536]{1,0:T(8,128)(2,1)}, u32[]{:S(2)}) copy-start(bf16[16,1536]{1,0:T(8,128)(2,1)} %design.1) | copy-start | bytes 147460
  2.7 0.8 %copy-start.1 = (f32[1536,8]{0,1:T(8,128)S(1)}, f32[1536,8]{0,1:T(8,128)}, u32[]{:S(2)}) copy-start(f32[1536,8]{0,1:T(8,128)} %param.7) | copy-start | bytes 147460
  3.5 0.7 %copy-start.2 = (f32[256]{0:T(256)S(1)}, f32[256]{0:T(256)}, u32[]{:S(2)}) copy-start(f32[256]{0:T(256)} %param.6) | copy-start | bytes 3076

commit v2 on v0

v2 whole, which is shorter than its diff:
```python
import jax
import jax.numpy as jnp
from jax import lax
from jax.experimental import pallas as pl
from jax.experimental.pallas import tpu as pltpu
from jax.sharding import PartitionSpec as P

MESH = pl.DeviceIdType.MESH
F32 = jnp.float32
BF16 = jnp.bfloat16
EPOCHS = 256
SIDE = 16
BLOCK = 16
WIDTH = 1536
LANES = 128
CHUNKS = WIDTH // LANES
STEP = 256
STEPS = WIDTH // STEP
GRANT = 54 << 20
FIRST = (((0,), (0,)), ((), ()))
LAST = (((1,), (1,)), ((), ()))


def owner_of(chunk):
    return (chunk // 3) * 4 + chunk % 3


def remote(src, dst, send, recv, device):
    return pltpu.make_async_remote_copy(
        src_ref=src, dst_ref=dst, send_sem=send, recv_sem=recv, device_id=device, device_id_type=MESH
    )


def split(value):
    high = value.astype(BF16)
    low = (value - high.astype(F32)).astype(BF16)
    return jnp.concatenate([high, low], axis=0)


def pair_sum(value):
    rows = value.shape[0] // 2
    return value[:rows] + value[rows:]


def squares_over_epochs(transposed):
    wide = transposed.astype(F32)
    parts = split(wide * wide)
    rows = transposed.shape[0]
    ones = jnp.ones((8, EPOCHS), BF16)
    both = lax.dot_general(ones, parts, LAST, preferred_element_type=F32)
    return both[:, :rows] + both[:, rows:] + 1e-06


def pack(value):
    return jnp.concatenate([value[:, :LANES], value[:, LANES:]], axis=0).astype(BF16)


def kernel(
    design_in, taps_in, probes_in, lower, upper,
    rt_out, c_out, answer_out,
    answer, design, taps, probes,
    cbuf, rsub, psub, filt, filt_t, white_rt, white_c, usend, ubuf, rs_send, rs_buf,
    in_sem, out_sem, c_send, c_recv, s_send, s_recv, p_send, p_recv, rs_ssem, rs_rsem,
    g_send, g_fwd, g_recv, u_send, u_recv,
):
    r, c = lax.axis_index("row"), lax.axis_index("col")
    h, z = r // 8, r % 8
    l, x, k = c // 8, (c // 2) % 4, c % 2
    sibling = (r, c + 1 - 2 * k)
    z_next, z_prev = (h * 8 + (z + 1) % 8, c), (h * 8 + (z + 7) % 8, c)
    partner = ((1 - h) * 8 + z, c)
    is_owner = c % 4 != 3
    mine = (c // 4) * 3 + c % 4
    on_diagonal = r == c

    loads = [
        pltpu.make_async_copy(src, dst, in_sem.at[i])
        for i, (src, dst) in enumerate(((design_in, design), (taps_in, taps), (probes_in, probes)))
    ]
    for load in loads:
        load.start()

    barrier = pltpu.get_barrier_semaphore()
    for o in range(1, SIDE):
        pl.semaphore_signal(barrier, inc=1, device_id=((r + o) % SIDE, r), device_id_type=MESH)

    @pl.when(jnp.logical_not(on_diagonal))
    def _():
        pl.semaphore_signal(barrier, inc=1, device_id=(r, r), device_id_type=MESH)

    for o in range(1, SIDE):
        pl.semaphore_signal(barrier, inc=1, device_id=((r + o) % SIDE, c), device_id_type=MESH)
    for o in range(1, SIDE):
        pl.semaphore_signal(barrier, inc=1, device_id=(r, (c + o) % SIDE), device_id_type=MESH)

    loads[1].wait()
    shape = (EPOCHS, EPOCHS)
    row_id = lax.broadcasted_iota(jnp.int32, shape, 0)
    col_id = lax.broadcasted_iota(jnp.int32, shape, 1)
    moved = jnp.broadcast_to(taps[...], shape)
    for bit in range(8):
        moved = jnp.where((row_id >> bit) % 2 == 1, pltpu.roll(moved, 1 << bit, 1), moved)
    moved = jnp.where(col_id >= row_id, moved, 0.0) + jnp.where(col_id == row_id, 1.0, 0.0)
    filt_t[...] = moved.astype(BF16)
    filt[...] = moved.T.astype(BF16)

    low = jnp.full((1, LANES), lower[0], F32)
    high = jnp.full((1, LANES), upper[0], F32)
    center = (low + high) / 2.0
    half = (high - low) / 2.0
    sigma = center / half
    rho0 = 1.0 / sigma
    rho1 = 1.0 / (2.0 * sigma - rho0)
    rho2 = 1.0 / (2.0 * sigma - rho1)

    def wide_row(row):
        return jnp.concatenate([row] * CHUNKS, axis=1)

    loads[0].wait()
    loads[2].wait()
    pl.semaphore_wait(barrier, 15 + 15 + 15 + jnp.where(on_diagonal, 0, 1))

    scatter = []
    for chunk in range(CHUNKS):
        owner = owner_of(chunk)
        copy = remote(
            design.at[:, pl.ds(chunk * LANES, LANES)], rsub.at[r], s_send.at[chunk], s_recv.at[r], (c, owner)
        )
        away = jnp.logical_not(jnp.logical_and(on_diagonal, c == owner))
        scatter.append((away, copy))

        @pl.when(away)
        def _():
            copy.start()

        @pl.when(jnp.logical_not(away))
        def _():
            rsub[r] = design[:, chunk * LANES : (chunk + 1) * LANES]

    def block_of(other, steps):
        return ((1 - h) if other else h) * 8 + (z + steps + 16) % 8

    sends = []

    def ship(slot, block, to, src=None):
        copy = remote(
            cbuf.at[block] if src is None else src, cbuf.at[block], c_send.at[slot], c_recv.at[block], to
        )
        copy.start()
        sends.append(copy)

    def await_block(block):
        remote(cbuf.at[block], cbuf.at[block], c_send.at[0], c_recv.at[block], z_next).wait_recv()

    way = 1 - 2 * h

    def at(steps):
        return (h * 8 + (z + steps + 8) % 8, c)

    ship(0, r, at(1), design)
    ship(1, r, at(-1), design)
    ship(2, r, partner, design)
    ship(3, r, at(2), design)
    ship(4, r, at(-2), design)
    for chunk in range(CHUNKS):
        owner = owner_of(chunk)
        copy = remote(
            probes.at[:, pl.ds(chunk * LANES, LANES)], psub.at[c], p_send.at[chunk], p_recv.at[c], (r, owner)
        )
        away = c != owner
        scatter.append((away, copy))

        @pl.when(away)
        def _():
            copy.start()

        @pl.when(jnp.logical_not(away))
        def _():
            psub[c] = probes[:, chunk * LANES : (chunk + 1) * LANES]

    cbuf[r] = design[...]

    await_block(block_of(True, 0))
    ship(5, block_of(True, 0), at(1))
    ship(6, block_of(True, 0), at(-1))
    ship(7, block_of(True, 0), at(2))
    ship(8, block_of(True, 0), at(-2))
    my_rows = pl.ds(pl.multiple_of(mine * LANES, LANES), LANES)

    @pl.when(is_owner)
    def _():
        for o in range(SIDE):
            source = (r + o) % SIDE

            def arrived():
                remote(rsub.at[source], rsub.at[source], s_send.at[0], s_recv.at[source], z_next).wait_recv()

            if o == 0:
                pl.when(jnp.logical_not(on_diagonal))(arrived)
            else:
                arrived()
        chunk_t = lax.dot_general(
            rsub[...].reshape(EPOCHS, LANES), filt_t[...], FIRST, preferred_element_type=F32
        ).astype(BF16)
        white_rt[my_rows, :] = chunk_t
        jacobi = squares_over_epochs(chunk_t)[:1]
        for o in range(1, SIDE):
            source = (c + o) % SIDE
            remote(psub.at[source], psub.at[source], p_send.at[0], p_recv.at[source], z_next).wait_recv()
        start = psub[...].reshape(SIDE * 8, LANES) / jacobi / center
        part = pair_sum(jnp.dot(split(start), chunk_t, preferred_element_type=F32))
        left = part[:, :LANES].reshape(SIDE, 8, LANES)
        right = part[:, LANES:].reshape(SIDE, 8, LANES)
        rs_send[...] = jnp.concatenate([left, right], axis=1).astype(BF16)
        for o in range(1, SIDE):
            to = (c + o) % SIDE
            remote(rs_send.at[to], rs_buf.at[mine], rs_ssem.at[o], rs_rsem.at[mine], (r, to)).start()
        rs_buf[mine] = rs_send[c]

    @pl.when(is_owner)
    def _():
        slot = 0
        for dl in range(2):
            for dx in range(4):
                to = sibling
                if dl or dx:
                    to = (r, ((l + dl) % 2) * 8 + ((x + dx) % 4) * 2 + k)
                remote(white_rt.at[my_rows], white_rt.at[my_rows], g_send.at[slot], g_recv.at[mine], to).start()
                slot += 1

    await_block(block_of(False, -2))
    ship(9, block_of(False, -2), at(1))
    await_block(block_of(False, 2))
    ship(10, block_of(False, 2), at(-1))
    ship(11, block_of(False, -2 * way), at(2 * way))
    await_block(block_of(True, -2))
    ship(12, block_of(True, -2), at(1))
    await_block(block_of(True, 2))
    ship(13, block_of(True, 2), at(-1))
    ship(14, block_of(True, 2 * way), at(-2 * way))
    def exchange_start(turn, packed):
        usend[turn] = packed
        ubuf[turn, r] = packed
        for o in range(1, SIDE):
            remote(
                usend.at[turn], ubuf.at[turn, r], u_send.at[turn, o], u_recv.at[turn, r], ((r + o) % SIDE, c)
            ).start()

    def exchange_finish(turn):
        for o in range(1, SIDE):
            source = (r + o) % SIDE
            slot = ubuf.at[turn, source]
            remote(slot, slot, u_send.at[turn, o], u_recv.at[turn, source], z_next).wait_recv()
        total = jnp.sum(ubuf[turn].astype(F32), axis=0)
        return split(jnp.concatenate([total[:8], total[8:]], axis=1))

    for chunk in range(CHUNKS):
        @pl.when(c != owner_of(chunk))
        def _():
            remote(
                rs_buf.at[chunk], rs_buf.at[chunk], rs_ssem.at[0], rs_rsem.at[chunk], sibling
            ).wait_recv()
    exchange_start(0, jnp.sum(rs_buf[...].astype(F32), axis=0).astype(BF16))

    forwards = []

    def chunk_copy(chunk):
        rows = white_rt.at[pl.ds(chunk * LANES, LANES)]
        return remote(rows, rows, g_fwd.at[chunk], g_recv.at[chunk], sibling)

    for chunk in range(CHUNKS):
        owner = owner_of(chunk)
        relay = jnp.logical_and(c != owner, k == owner % 2)
        copy = chunk_copy(chunk)
        forwards.append((relay, copy))

        @pl.when(relay)
        def _():
            copy.wait_recv()
            copy.start()

    for chunk in range(CHUNKS):
        @pl.when(k != owner_of(chunk) % 2)
        def _():
            chunk_copy(chunk).wait_recv()

    def back_product(whole):
        return pair_sum(lax.dot_general(whole, white_rt[...], LAST, preferred_element_type=F32))

    leave_rt = pltpu.make_async_copy(white_rt, rt_out, out_sem.at[0])
    leave_rt.start()
    jacobi = squares_over_epochs(white_rt[...])
    direction0 = probes[...] / jacobi / wide_row(center)
    residual1 = probes[...] - back_product(exchange_finish(0))
    direction1 = wide_row(rho1 * rho0) * direction0 + wide_row(2.0 * rho1 / half) * (residual1 / jacobi)
    exchange_start(
        1, pack(pair_sum(jnp.dot(split(direction1), white_rt[...], preferred_element_type=F32)))
    )

    for other in (False, True):
        for steps in (-3, -1, 1, 3, 4):
            await_block(block_of(other, steps))
    white_c[...] = jnp.dot(
        filt[...], cbuf[...].reshape(EPOCHS, WIDTH), preferred_element_type=F32
    ).astype(BF16)

    leave_c = pltpu.make_async_copy(white_c, c_out, out_sem.at[1])
    leave_c.start()

    residual2 = residual1 - back_product(exchange_finish(1))
    direction2 = wide_row(rho2 * rho1) * direction1 + wide_row(2.0 * rho2 / half) * (residual2 / jacobi)
    answer[...] = direction0 + direction1 + direction2
    leave_answer = pltpu.make_async_copy(answer, answer_out, out_sem.at[2])
    leave_answer.start()

    for copy in sends:
        copy.wait_send()
    for away, copy in scatter + forwards:
        pl.when(away)(copy.wait_send)
    for turn in range(2):
        for o in range(1, SIDE):
            remote(
                usend.at[turn], ubuf.at[turn, r], u_send.at[turn, o], u_recv.at[turn, r], z_next
            ).wait_send()

    @pl.when(is_owner)
    def _():
        for o in range(1, SIDE):
            remote(rs_send.at[0], rs_buf.at[mine], rs_ssem.at[o], rs_rsem.at[mine], z_next).wait_send()
        for slot in range(8):
            remote(white_rt.at[my_rows], white_rt.at[my_rows], g_send.at[slot], g_recv.at[mine], sibling).wait_send()

    leave_rt.wait()
    leave_c.wait()
    leave_answer.wait()


def tile_kernel(rt_in, c_in, answer_in, tile_out, answer_out, white_rt, white_c, answer, rows, in_sem, out_sem):
    load_c = pltpu.make_async_copy(c_in, white_c, in_sem.at[0])
    load_c.start()
    loads, leaves = [], []
    for part in range(STEPS):
        here = pl.ds(part * STEP, STEP)
        loads.append(pltpu.make_async_copy(rt_in.at[here], white_rt.at[here], in_sem.at[2 + part]))
        leaves.append(pltpu.make_async_copy(rows.at[part], tile_out.at[here], out_sem.at[1 + part]))
        loads[part].start()
    load_answer = pltpu.make_async_copy(answer_in, answer, in_sem.at[1])
    load_answer.start()
    load_c.wait()
    for part in range(STEPS):
        loads[part].wait()
        rows[part] = jnp.dot(
            white_rt[part * STEP : (part + 1) * STEP], white_c[...], preferred_element_type=F32
        )
        leaves[part].start()
    load_answer.wait()
    leave_answer = pltpu.make_async_copy(answer, answer_out, out_sem.at[0])
    leave_answer.start()
    for leave in leaves:
        leave.wait()
    leave_answer.wait()


def body(design, filter_taps, probes, lower_bound, upper_bound):
    smem = pl.BlockSpec(memory_space=pltpu.SMEM)
    hbm = pl.BlockSpec(memory_space=pltpu.HBM)
    dma = pltpu.SemaphoreType.DMA
    white_rt, white_c, answer = pl.pallas_call(
        kernel,
        out_shape=(
            jax.ShapeDtypeStruct((WIDTH, EPOCHS), BF16),
            jax.ShapeDtypeStruct((EPOCHS, WIDTH), BF16),
            jax.ShapeDtypeStruct((8, WIDTH), F32),
        ),
        in_specs=[hbm, hbm, hbm, smem, smem],
        out_specs=(hbm, hbm, hbm),
        scratch_shapes=[
            pltpu.VMEM((8, WIDTH), F32),
            pltpu.VMEM((BLOCK, WIDTH), BF16),
            pltpu.VMEM((1, EPOCHS), F32),
            pltpu.VMEM((8, WIDTH), F32),
            pltpu.VMEM((SIDE, BLOCK, WIDTH), BF16),
            pltpu.VMEM((SIDE, BLOCK, LANES), BF16),
            pltpu.VMEM((SIDE, 8, LANES), F32),
            pltpu.VMEM((EPOCHS, EPOCHS), BF16),
            pltpu.VMEM((EPOCHS, EPOCHS), BF16),
            pltpu.VMEM((WIDTH, EPOCHS), BF16),
            pltpu.VMEM((EPOCHS, WIDTH), BF16),
            pltpu.VMEM((2, 16, LANES), BF16),
            pltpu.VMEM((2, SIDE, 16, LANES), BF16),
            pltpu.VMEM((SIDE, 16, LANES), BF16),
            pltpu.VMEM((CHUNKS, 16, LANES), BF16),
            dma((3,)), dma((3,)),
            dma((15,)), dma((SIDE,)),
            dma((CHUNKS,)), dma((SIDE,)),
            dma((CHUNKS,)), dma((SIDE,)),
            dma((SIDE,)), dma((CHUNKS,)),
            dma((8,)), dma((CHUNKS,)), dma((CHUNKS,)),
            dma((2, SIDE)), dma((2, SIDE)),
        ],
        compiler_params=pltpu.CompilerParams(
            collective_id=1, has_side_effects=True, vmem_limit_bytes=GRANT
        ),
        name="gather_and_solve",
    )(design, filter_taps.reshape(1, EPOCHS), probes.T, lower_bound, upper_bound)
    tile, answer = pl.pallas_call(
        tile_kernel,
        out_shape=(
            jax.ShapeDtypeStruct((WIDTH, WIDTH), F32),
            jax.ShapeDtypeStruct((8, WIDTH), F32),
        ),
        in_specs=[hbm, hbm, hbm],
        out_specs=(hbm, hbm),
        scratch_shapes=[
            pltpu.VMEM((WIDTH, EPOCHS), BF16),
            pltpu.VMEM((EPOCHS, WIDTH), BF16),
            pltpu.VMEM((8, WIDTH), F32),
            pltpu.VMEM((STEPS, STEP, WIDTH), F32),
            dma((2 + STEPS,)), dma((1 + STEPS,)),
        ],
        compiler_params=pltpu.CompilerParams(vmem_limit_bytes=GRANT),
        name="normal_tile",
    )(white_rt, white_c, answer)
    return tile, answer.T


def solution(mesh):
    placed = (P("row", "col"), P(), P("row", "col"), P(), P())
    return jax.shard_map(
        body,
        mesh=mesh,
        in_specs=placed,
        out_specs=(P("row", "col"), P("row", "col")),
        check_vma=False,
    )
```

time: 762 us -> 48.5 us (0.06)
  waiting for transfers between devices: 643 us -> 0 us
  blocking collectives: 71.8 us -> 0 us
  Pallas kernels: 0 us -> 46.4 us
  matrix products: 22.9 us -> 0 us
  between operations: 15.4 us -> 1.93 us
    psum x5 -> x0, waiting for transfers between devices: 643 us -> none  [the longest x3 384 us: broadcast(): return lax.psum(block, axis)]
    all_gather x2 -> x0, blocking collectives: 71.8 us -> none  [the longest x1 42.2 us: body(): whole_panel = lax.all_gather(design, 'row', axis=0, tiled=True)]
    pallas_call x0 -> x2, Pallas kernels: none -> 46.4 us  [the longest x1 41.2 us: body(): pl.pallas_call(kernel, out_shape=(jax.ShapeDtypeStruct((WIDTH, EPOCHS), B...]
    dot_general x4 -> x0, matrix products: 22.9 us -> none  [the longest x2 15.4 us: tile_product(): partial_sum = jnp.dot(normal_tile, piece, precision=lax.Precision.HIGHEST)]
  transfers between devices with their start and end apart: 5 -> 0, of which waited for: 5 -> 0; matrix products, arithmetic and copies ran while one was open for 1% -> 0% of each run, Pallas kernels for 0% -> 0%
where the time goes in v2:
time: 48.5 us; the launch traced here: 48.4 us
  Pallas kernels  46.4 us (96%)
  between operations  1.93 us (4%)
    pallas_call x1, Pallas kernels, body(): pl.pallas_call(kernel, out_shape=(jax.ShapeDtypeStruct((WIDTH, EPOCHS), B...  41.2 us
    pallas_call x1, Pallas kernels, body(): pl.pallas_call(tile_kernel, out_shape=(jax.ShapeDtypeStruct((WIDTH, WIDTH...  5.29 us

profile of v2, /device:TPU:1, one launch (start us, length us, event | category | flops | bytes accessed | tf_op | source)
XLA Modules:
  0.0 48.4 jit_solution(17440865135205798555)
XLA Ops:
  1.9 41.2 %gather_and_solve.1 = (bf16[1536,256]{1,0:T(8,128)(2,1)}, bf16[256,1536]{1,0:T(8,128)(2,1)}, f32[8,1536]{1,0:T(8,128)}) custom-call(bf16[16,1536]{1,0:T(8,128)(2,1)} %design_in.1, f32[1,256]{1,0:T(1,128)} %bitcast.4, f32[8,1536]{1,0:T(8,128)} %bitcast.3, f32[1]{0:T(128)S(6)} %copy.7.lower, f32[1]{0:T(128)S(6)} %copy.8.upper), custom_call_target="tpu_custom_call" | custom-call | tf_op jit(solution)/shard_map/gather_and_solve/pallas_call | solution.py:368
  43.1 5.3 %normal_tile.1 = (f32[1536,1536]{1,0:T(8,128)}, f32[8,1536]{1,0:T(8,128)}) custom-call(bf16[1536,256]{1,0:T(8,128)(2,1)} %get-tuple-element.7.rt_in, bf16[256,1536]{1,0:T(8,128)(2,1)} %get-tuple-element.8.c_in, f32[8,1536]{1,0:T(8,128)} %get-tuple-element.9.answer_in), custom_call_target="tpu_custom_call" | custom-call | tf_op jit(solution)/shard_map/normal_tile/pallas_call | solution.py:406

commit v3 on v2

--- a/solution.py
+++ b/solution.py
@@ -25,6 +25,15 @@
     return (chunk // 3) * 4 + chunk % 3
 
 
+PLANE = tuple(sorted(((a, b) for a in range(2) for b in range(8) if a or b), key=lambda p: -(2 * p[0] + min(p[1], 8 - p[1]))))
+ROW = tuple(
+    sorted(
+        ((a, b, d) for a in range(2) for b in range(4) for d in range(2) if a or b or d),
+        key=lambda p: -(2 * (p[0] + min(p[1], 4 - p[1])) + p[2]),
+    )
+)
+
+
 def remote(src, dst, send, recv, device):
     return pltpu.make_async_remote_copy(
         src_ref=src, dst_ref=dst, send_sem=send, recv_sem=recv, device_id=device, device_id_type=MESH
@@ -55,10 +64,14 @@
     return jnp.concatenate([value[:, :LANES], value[:, LANES:]], axis=0).astype(BF16)
 
 
+def back_product(whole, transposed):
+    return pair_sum(lax.dot_general(whole, transposed, LAST, preferred_element_type=F32))
+
+
 def kernel(
     design_in, taps_in, probes_in, lower, upper,
-    rt_out, c_out, answer_out,
-    answer, design, taps, probes,
+    rt_out, c_out, state_out, last_out,
+    state, last, design, taps, probes,
     cbuf, rsub, psub, filt, filt_t, white_rt, white_c, usend, ubuf, rs_send, rs_buf,
     in_sem, out_sem, c_send, c_recv, s_send, s_recv, p_send, p_recv, rs_ssem, rs_rsem,
     g_send, g_fwd, g_recv, u_send, u_recv,
@@ -73,6 +86,12 @@
     mine = (c // 4) * 3 + c % 4
     on_diagonal = r == c
 
+    def in_plane(place):
+        return ((h + place[0]) % 2) * 8 + (z + place[1]) % 8
+
+    def in_row(place):
+        return ((l + place[0]) % 2) * 8 + ((x + place[1]) % 4) * 2 + (k + place[2]) % 2
+
     loads = [
         pltpu.make_async_copy(src, dst, in_sem.at[i])
         for i, (src, dst) in enumerate(((design_in, design), (taps_in, taps), (probes_in, probes)))
@@ -88,10 +107,10 @@
     def _():
         pl.semaphore_signal(barrier, inc=1, device_id=(r, r), device_id_type=MESH)
 
-    for o in range(1, SIDE):
-        pl.semaphore_signal(barrier, inc=1, device_id=((r + o) % SIDE, c), device_id_type=MESH)
-    for o in range(1, SIDE):
-        pl.semaphore_signal(barrier, inc=1, device_id=(r, (c + o) % SIDE), device_id_type=MESH)
+    for place in PLANE:
+        pl.semaphore_signal(barrier, inc=1, device_id=(in_plane(place), c), device_id_type=MESH)
+    for place in ROW:
+        pl.semaphore_signal(barrier, inc=1, device_id=(r, in_row(place)), device_id_type=MESH)
 
     loads[1].wait()
     shape = (EPOCHS, EPOCHS)
@@ -113,6 +132,9 @@
     rho1 = 1.0 / (2.0 * sigma - rho0)
     rho2 = 1.0 / (2.0 * sigma - rho1)
 
+    def await_bytes(ref, sem):
+        pltpu.make_async_copy(ref, ref, sem).wait()
+
     def wide_row(row):
         return jnp.concatenate([row] * CHUNKS, axis=1)
 
@@ -120,14 +142,12 @@
     loads[2].wait()
     pl.semaphore_wait(barrier, 15 + 15 + 15 + jnp.where(on_diagonal, 0, 1))
 
-    scatter = []
     for chunk in range(CHUNKS):
         owner = owner_of(chunk)
         copy = remote(
-            design.at[:, pl.ds(chunk * LANES, LANES)], rsub.at[r], s_send.at[chunk], s_recv.at[r], (c, owner)
+            design.at[:, pl.ds(chunk * LANES, LANES)], rsub.at[r], s_send, s_recv, (c, owner)
         )
         away = jnp.logical_not(jnp.logical_and(on_diagonal, c == owner))
-        scatter.append((away, copy))
 
         @pl.when(away)
         def _():
@@ -165,10 +185,9 @@
     for chunk in range(CHUNKS):
         owner = owner_of(chunk)
         copy = remote(
-            probes.at[:, pl.ds(chunk * LANES, LANES)], psub.at[c], p_send.at[chunk], p_recv.at[c], (r, owner)
+            probes.at[:, pl.ds(chunk * LANES, LANES)], psub.at[c], p_send, p_recv, (r, owner)
         )
         away = c != owner
-        scatter.append((away, copy))
 
         @pl.when(away)
         def _():
@@ -189,44 +208,36 @@
 
     @pl.when(is_owner)
     def _():
-        for o in range(SIDE):
-            source = (r + o) % SIDE
-
-            def arrived():
-                remote(rsub.at[source], rsub.at[source], s_send.at[0], s_recv.at[source], z_next).wait_recv()
-
-            if o == 0:
-                pl.when(jnp.logical_not(on_diagonal))(arrived)
-            else:
-                arrived()
-        chunk_t = lax.dot_general(
-            rsub[...].reshape(EPOCHS, LANES), filt_t[...], FIRST, preferred_element_type=F32
-        ).astype(BF16)
-        white_rt[my_rows, :] = chunk_t
-        jacobi = squares_over_epochs(chunk_t)[:1]
-        for o in range(1, SIDE):
-            source = (c + o) % SIDE
-            remote(psub.at[source], psub.at[source], p_send.at[0], p_recv.at[source], z_next).wait_recv()
-        start = psub[...].reshape(SIDE * 8, LANES) / jacobi / center
-        part = pair_sum(jnp.dot(split(start), chunk_t, preferred_element_type=F32))
+        await_bytes(psub.at[pl.ds(0, SIDE - 1)], p_recv)
+        right = psub[...].reshape(SIDE * 8, LANES) / center
+
+        @pl.when(on_diagonal)
+        def _():
+            await_bytes(rsub.at[pl.ds(0, SIDE - 1)], s_recv)
+
+        @pl.when(jnp.logical_not(on_diagonal))
+        def _():
+            await_bytes(rsub, s_recv)
+
+        raw = rsub[...].reshape(EPOCHS, LANES)
+        chunk_t = lax.dot_general(raw, filt_t[...], FIRST, preferred_element_type=F32).astype(BF16)
+        wide = jnp.dot(filt[...], raw, preferred_element_type=F32).astype(BF16).astype(F32)
+        jacobi = jnp.sum(wide * wide, axis=0, keepdims=True) + 1e-06
+        part = pair_sum(jnp.dot(split(right / jacobi), chunk_t, preferred_element_type=F32))
         left = part[:, :LANES].reshape(SIDE, 8, LANES)
         right = part[:, LANES:].reshape(SIDE, 8, LANES)
         rs_send[...] = jnp.concatenate([left, right], axis=1).astype(BF16)
-        for o in range(1, SIDE):
-            to = (c + o) % SIDE
-            remote(rs_send.at[to], rs_buf.at[mine], rs_ssem.at[o], rs_rsem.at[mine], (r, to)).start()
+        for place in ROW:
+            to = in_row(place)
+            remote(rs_send.at[to], rs_buf.at[mine], rs_ssem, rs_rsem, (r, to)).start()
         rs_buf[mine] = rs_send[c]
-
-    @pl.when(is_owner)
-    def _():
-        slot = 0
-        for dl in range(2):
-            for dx in range(4):
-                to = sibling
-                if dl or dx:
-                    to = (r, ((l + dl) % 2) * 8 + ((x + dx) % 4) * 2 + k)
-                remote(white_rt.at[my_rows], white_rt.at[my_rows], g_send.at[slot], g_recv.at[mine], to).start()
-                slot += 1
+        white_rt[my_rows, :] = chunk_t
+        for place in ROW:
+            if not place[2]:
+                remote(
+                    white_rt.at[my_rows], white_rt.at[my_rows], g_send, g_recv.at[mine], (r, in_row(place))
+                ).start()
+        remote(white_rt.at[my_rows], white_rt.at[my_rows], g_send, g_recv.at[mine], sibling).start()
 
     await_block(block_of(False, -2))
     ship(9, block_of(False, -2), at(1))
@@ -241,25 +252,24 @@
     def exchange_start(turn, packed):
         usend[turn] = packed
         ubuf[turn, r] = packed
-        for o in range(1, SIDE):
+        for place in PLANE:
             remote(
-                usend.at[turn], ubuf.at[turn, r], u_send.at[turn, o], u_recv.at[turn, r], ((r + o) % SIDE, c)
+                usend.at[turn], ubuf.at[turn, r], u_send.at[turn], u_recv.at[turn], (in_plane(place), c)
             ).start()
 
     def exchange_finish(turn):
-        for o in range(1, SIDE):
-            source = (r + o) % SIDE
-            slot = ubuf.at[turn, source]
-            remote(slot, slot, u_send.at[turn, o], u_recv.at[turn, source], z_next).wait_recv()
+        await_bytes(ubuf.at[turn, pl.ds(0, SIDE - 1)], u_recv.at[turn])
         total = jnp.sum(ubuf[turn].astype(F32), axis=0)
         return split(jnp.concatenate([total[:8], total[8:]], axis=1))
 
-    for chunk in range(CHUNKS):
-        @pl.when(c != owner_of(chunk))
-        def _():
-            remote(
-                rs_buf.at[chunk], rs_buf.at[chunk], rs_ssem.at[0], rs_rsem.at[chunk], sibling
-            ).wait_recv()
+    @pl.when(is_owner)
+    def _():
+        await_bytes(rs_buf.at[pl.ds(0, CHUNKS - 1)], rs_rsem)
+
+    @pl.when(jnp.logical_not(is_owner))
+    def _():
+        await_bytes(rs_buf, rs_rsem)
+
     exchange_start(0, jnp.sum(rs_buf[...].astype(F32), axis=0).astype(BF16))
 
     forwards = []
@@ -284,14 +294,11 @@
         def _():
             chunk_copy(chunk).wait_recv()
 
-    def back_product(whole):
-        return pair_sum(lax.dot_general(whole, white_rt[...], LAST, preferred_element_type=F32))
-
     leave_rt = pltpu.make_async_copy(white_rt, rt_out, out_sem.at[0])
     leave_rt.start()
     jacobi = squares_over_epochs(white_rt[...])
     direction0 = probes[...] / jacobi / wide_row(center)
-    residual1 = probes[...] - back_product(exchange_finish(0))
+    residual1 = probes[...] - back_product(exchange_finish(0), white_rt[...])
     direction1 = wide_row(rho1 * rho0) * direction0 + wide_row(2.0 * rho1 / half) * (residual1 / jacobi)
     exchange_start(
         1, pack(pair_sum(jnp.dot(split(direction1), white_rt[...], preferred_element_type=F32)))
@@ -307,45 +314,65 @@
     leave_c = pltpu.make_async_copy(white_c, c_out, out_sem.at[1])
     leave_c.start()
 
-    residual2 = residual1 - back_product(exchange_finish(1))
-    direction2 = wide_row(rho2 * rho1) * direction1 + wide_row(2.0 * rho2 / half) * (residual2 / jacobi)
-    answer[...] = direction0 + direction1 + direction2
-    leave_answer = pltpu.make_async_copy(answer, answer_out, out_sem.at[2])
-    leave_answer.start()
+    state[0] = residual1
+    state[1] = wide_row(2.0 * rho2 / half) / jacobi
+    state[2] = direction0 + direction1 + wide_row(rho2 * rho1) * direction1
+    leave_state = pltpu.make_async_copy(state, state_out, out_sem.at[2])
+    leave_state.start()
 
     for copy in sends:
         copy.wait_send()
-    for away, copy in scatter + forwards:
-        pl.when(away)(copy.wait_send)
-    for turn in range(2):
-        for o in range(1, SIDE):
-            remote(
-                usend.at[turn], ubuf.at[turn, r], u_send.at[turn, o], u_recv.at[turn, r], z_next
-            ).wait_send()
+    for relay, copy in forwards:
+        pl.when(relay)(copy.wait_send)
 
     @pl.when(is_owner)
     def _():
-        for o in range(1, SIDE):
-            remote(rs_send.at[0], rs_buf.at[mine], rs_ssem.at[o], rs_rsem.at[mine], z_next).wait_send()
-        for slot in range(8):
-            remote(white_rt.at[my_rows], white_rt.at[my_rows], g_send.at[slot], g_recv.at[mine], sibling).wait_send()
-
+        await_bytes(rs_send.at[pl.ds(0, SIDE - 1)], rs_ssem)
+        await_bytes(white_rt.at[pl.ds(0, 8 * LANES)], g_send)
+        await_bytes(probes.at[:, pl.ds(0, WIDTH - LANES)], p_send)
+
+    @pl.when(jnp.logical_not(is_owner))
+    def _():
+        await_bytes(probes, p_send)
+
+    kept = jnp.logical_and(is_owner, on_diagonal)
+
+    @pl.when(kept)
+    def _():
+        await_bytes(design.at[:, pl.ds(0, WIDTH - LANES)], s_send)
+
+    @pl.when(jnp.logical_not(kept))
+    def _():
+        await_bytes(design, s_send)
+
+    await_bytes(ubuf.at[0, pl.ds(0, SIDE - 1)], u_send.at[0])
     leave_rt.wait()
     leave_c.wait()
-    leave_answer.wait()
-
-
-def tile_kernel(rt_in, c_in, answer_in, tile_out, answer_out, white_rt, white_c, answer, rows, in_sem, out_sem):
+    leave_state.wait()
+
+    last[...] = exchange_finish(1)
+    leave_last = pltpu.make_async_copy(last, last_out, out_sem.at[3])
+    leave_last.start()
+    await_bytes(ubuf.at[1, pl.ds(0, SIDE - 1)], u_send.at[1])
+    leave_last.wait()
+
+
+def tile_kernel(
+    rt_in, c_in, state_in, last_in, tile_out, answer_out,
+    white_rt, white_c, state, last, answer, rows, in_sem, out_sem,
+):
     load_c = pltpu.make_async_copy(c_in, white_c, in_sem.at[0])
     load_c.start()
     loads, leaves = [], []
     for part in range(STEPS):
         here = pl.ds(part * STEP, STEP)
-        loads.append(pltpu.make_async_copy(rt_in.at[here], white_rt.at[here], in_sem.at[2 + part]))
+        loads.append(pltpu.make_async_copy(rt_in.at[here], white_rt.at[here], in_sem.at[3 + part]))
         leaves.append(pltpu.make_async_copy(rows.at[part], tile_out.at[here], out_sem.at[1 + part]))
         loads[part].start()
-    load_answer = pltpu.make_async_copy(answer_in, answer, in_sem.at[1])
-    load_answer.start()
+    load_state = pltpu.make_async_copy(state_in, state, in_sem.at[1])
+    load_last = pltpu.make_async_copy(last_in, last, in_sem.at[2])
+    load_state.start()
+    load_last.start()
     load_c.wait()
     for part in range(STEPS):
         loads[part].wait()
@@ -353,7 +380,10 @@
             white_rt[part * STEP : (part + 1) * STEP], white_c[...], preferred_element_type=F32
         )
         leaves[part].start()
-    load_answer.wait()
+    load_state.wait()
+    load_last.wait()
+    residual2 = state[0] - back_product(last[...], white_rt[...])
+    answer[...] = state[2] + state[1] * residual2
     leave_answer = pltpu.make_async_copy(answer, answer_out, out_sem.at[0])
     leave_answer.start()
     for leave in leaves:
@@ -365,17 +395,19 @@
     smem = pl.BlockSpec(memory_space=pltpu.SMEM)
     hbm = pl.BlockSpec(memory_space=pltpu.HBM)
     dma = pltpu.SemaphoreType.DMA
-    white_rt, white_c, answer = pl.pallas_call(
+    held = pl.pallas_call(
         kernel,
         out_shape=(
             jax.ShapeDtypeStruct((WIDTH, EPOCHS), BF16),
             jax.ShapeDtypeStruct((EPOCHS, WIDTH), BF16),
-            jax.ShapeDtypeStruct((8, WIDTH), F32),
+            jax.ShapeDtypeStruct((3, 8, WIDTH), F32),
+            jax.ShapeDtypeStruct((16, EPOCHS), BF16),
         ),
         in_specs=[hbm, hbm, hbm, smem, smem],
-        out_specs=(hbm, hbm, hbm),
+        out_specs=(hbm, hbm, hbm, hbm),
         scratch_shapes=[
-            pltpu.VMEM((8, WIDTH), F32),
+            pltpu.VMEM((3, 8, WIDTH), F32),
+            pltpu.VMEM((16, EPOCHS), BF16),
             pltpu.VMEM((BLOCK, WIDTH), BF16),
             pltpu.VMEM((1, EPOCHS), F32),
             pltpu.VMEM((8, WIDTH), F32),
@@ -390,13 +422,13 @@
             pltpu.VMEM((2, SIDE, 16, LANES), BF16),
             pltpu.VMEM((SIDE, 16, LANES), BF16),
             pltpu.VMEM((CHUNKS, 16, LANES), BF16),
-            dma((3,)), dma((3,)),
+            dma((3,)), dma((4,)),
             dma((15,)), dma((SIDE,)),
-            dma((CHUNKS,)), dma((SIDE,)),
-            dma((CHUNKS,)), dma((SIDE,)),
-            dma((SIDE,)), dma((CHUNKS,)),
-            dma((8,)), dma((CHUNKS,)), dma((CHUNKS,)),
-            dma((2, SIDE)), dma((2, SIDE)),
+            dma, dma,
+            dma, dma,
+            dma, dma,
+            dma, dma((CHUNKS,)), dma((CHUNKS,)),
+            dma((2,)), dma((2,)),
         ],
         compiler_params=pltpu.CompilerParams(
             collective_id=1, has_side_effects=True, vmem_limit_bytes=GRANT
@@ -409,18 +441,20 @@
             jax.ShapeDtypeStruct((WIDTH, WIDTH), F32),
             jax.ShapeDtypeStruct((8, WIDTH), F32),
         ),
-        in_specs=[hbm, hbm, hbm],
+        in_specs=[hbm] * 4,
         out_specs=(hbm, hbm),
         scratch_shapes=[
             pltpu.VMEM((WIDTH, EPOCHS), BF16),
             pltpu.VMEM((EPOCHS, WIDTH), BF16),
+            pltpu.VMEM((3, 8, WIDTH), F32),
+            pltpu.VMEM((16, EPOCHS), BF16),
             pltpu.VMEM((8, WIDTH), F32),
             pltpu.VMEM((STEPS, STEP, WIDTH), F32),
-            dma((2 + STEPS,)), dma((1 + STEPS,)),
+            dma((3 + STEPS,)), dma((1 + STEPS,)),
         ],
         compiler_params=pltpu.CompilerParams(vmem_limit_bytes=GRANT),
         name="normal_tile",
-    )(white_rt, white_c, answer)
+    )(*held)
     return tile, answer.T
 
 

time: 48.5 us -> 44.6 us (0.920)
  Pallas kernels: 46.4 us -> 42.5 us
    pallas_call x1, Pallas kernels: 41.2 us -> 37.2 us  [body(): pl.pallas_call(kernel, out_shape=(jax.ShapeDtypeStruct((WIDTH, EPOCHS), B...]
where the time goes in v3:
time: 44.6 us; the launch traced here: 44.4 us
  Pallas kernels  42.5 us (95%)
  between operations  1.93 us (4%)
    pallas_call x1, Pallas kernels, body(): pl.pallas_call(kernel, out_shape=(jax.ShapeDtypeStruct((WIDTH, EPOCHS), B...  37.2 us
    pallas_call x1, Pallas kernels, body(): pl.pallas_call(tile_kernel, out_shape=(jax.ShapeDtypeStruct((WIDTH, WIDTH...  5.3 us

profile of v3, /device:TPU:1, one launch (start us, length us, event | category | flops | bytes accessed | tf_op | source)
XLA Modules:
  0.0 44.4 jit_solution(3877438813312899849)
XLA Ops:
  1.9 37.2 %gather_and_solve.1 = (bf16[1536,256]{1,0:T(8,128)(2,1)}, bf16[256,1536]{1,0:T(8,128)(2,1)}, f32[3,8,1536]{2,1,0:T(8,128)}, bf16[16,256]{1,0:T(8,128)(2,1)}) custom-call(bf16[16,1536]{1,0:T(8,128)(2,1)} %design_in.1, f32[1,256]{1,0:T(1,128)} %bitcast.4, f32[8,1536]{1,0:T(8,128)} %bitcast.3, f32[1]{0:T(128)S(6)} %copy.7.lower, f32[1]{0:T(128)S(6)} %copy.8.upper), custom_call_target="tpu_custom_call" | custom-call | tf_op jit(solution)/shard_map/gather_and_solve/pallas_call | solution.py:398
  39.1 5.3 %normal_tile.1 = (f32[1536,1536]{1,0:T(8,128)}, f32[8,1536]{1,0:T(8,128)}) custom-call(bf16[1536,256]{1,0:T(8,128)(2,1)} %get-tuple-element.8.rt_in, bf16[256,1536]{1,0:T(8,128)(2,1)} %get-tuple-element.9.c_in, f32[3,8,1536]{2,1,0:T(8,128)} %get-tuple-element.10.state_in, bf16[16,256]{1,0:T(8,128)(2,1)} %get-tuple-element.11.last_in), custom_call_target="tpu_custom_call" | custom-call | tf_op jit(solution)/shard_map/normal_tile/pallas_call | solution.py:438

commit v4 on v3

--- a/solution.py
+++ b/solution.py
@@ -68,10 +68,15 @@
     return pair_sum(lax.dot_general(whole, transposed, LAST, preferred_element_type=F32))
 
 
+def plane_sum(slots):
+    total = jnp.sum(slots.astype(F32), axis=0)
+    return split(jnp.concatenate([total[:8], total[8:]], axis=1))
+
+
 def kernel(
     design_in, taps_in, probes_in, lower, upper,
     rt_out, c_out, state_out, last_out,
-    state, last, design, taps, probes,
+    state, design, taps, probes,
     cbuf, rsub, psub, filt, filt_t, white_rt, white_c, usend, ubuf, rs_send, rs_buf,
     in_sem, out_sem, c_send, c_recv, s_send, s_recv, p_send, p_recv, rs_ssem, rs_rsem,
     g_send, g_fwd, g_recv, u_send, u_recv,
@@ -100,8 +105,8 @@
         load.start()
 
     barrier = pltpu.get_barrier_semaphore()
-    for o in range(1, SIDE):
-        pl.semaphore_signal(barrier, inc=1, device_id=((r + o) % SIDE, r), device_id_type=MESH)
+    for place in PLANE:
+        pl.semaphore_signal(barrier, inc=1, device_id=(in_plane(place), r), device_id_type=MESH)
 
     @pl.when(jnp.logical_not(on_diagonal))
     def _():
@@ -249,19 +254,13 @@
     await_block(block_of(True, 2))
     ship(13, block_of(True, 2), at(-1))
     ship(14, block_of(True, 2 * way), at(-2 * way))
-    def exchange_start(turn, packed):
+    def exchange_start(turn, packed, slots):
         usend[turn] = packed
-        ubuf[turn, r] = packed
         for place in PLANE:
             remote(
-                usend.at[turn], ubuf.at[turn, r], u_send.at[turn], u_recv.at[turn], (in_plane(place), c)
+                usend.at[turn], slots.at[r], u_send.at[turn], u_recv.at[turn], (in_plane(place), c)
             ).start()
 
-    def exchange_finish(turn):
-        await_bytes(ubuf.at[turn, pl.ds(0, SIDE - 1)], u_recv.at[turn])
-        total = jnp.sum(ubuf[turn].astype(F32), axis=0)
-        return split(jnp.concatenate([total[:8], total[8:]], axis=1))
-
     @pl.when(is_owner)
     def _():
         await_bytes(rs_buf.at[pl.ds(0, CHUNKS - 1)], rs_rsem)
@@ -270,7 +269,9 @@
     def _():
         await_bytes(rs_buf, rs_rsem)
 
-    exchange_start(0, jnp.sum(rs_buf[...].astype(F32), axis=0).astype(BF16))
+    summed = jnp.sum(rs_buf[...].astype(F32), axis=0).astype(BF16)
+    exchange_start(0, summed, ubuf)
+    ubuf[r] = summed
 
     forwards = []
 
@@ -298,11 +299,14 @@
     leave_rt.start()
     jacobi = squares_over_epochs(white_rt[...])
     direction0 = probes[...] / jacobi / wide_row(center)
-    residual1 = probes[...] - back_product(exchange_finish(0), white_rt[...])
+    await_bytes(ubuf.at[pl.ds(0, SIDE - 1)], u_recv.at[0])
+    residual1 = probes[...] - back_product(plane_sum(ubuf[...]), white_rt[...])
     direction1 = wide_row(rho1 * rho0) * direction0 + wide_row(2.0 * rho1 / half) * (residual1 / jacobi)
     exchange_start(
-        1, pack(pair_sum(jnp.dot(split(direction1), white_rt[...], preferred_element_type=F32)))
+        1, pack(pair_sum(jnp.dot(split(direction1), white_rt[...], preferred_element_type=F32))), last_out
     )
+    keep_last = pltpu.make_async_copy(usend.at[1], last_out.at[r], out_sem.at[3])
+    keep_last.start()
 
     for other in (False, True):
         for steps in (-3, -1, 1, 3, 4):
@@ -345,16 +349,14 @@
     def _():
         await_bytes(design, s_send)
 
-    await_bytes(ubuf.at[0, pl.ds(0, SIDE - 1)], u_send.at[0])
+    await_bytes(ubuf.at[pl.ds(0, SIDE - 1)], u_send.at[0])
     leave_rt.wait()
     leave_c.wait()
     leave_state.wait()
 
-    last[...] = exchange_finish(1)
-    leave_last = pltpu.make_async_copy(last, last_out, out_sem.at[3])
-    leave_last.start()
-    await_bytes(ubuf.at[1, pl.ds(0, SIDE - 1)], u_send.at[1])
-    leave_last.wait()
+    keep_last.wait()
+    await_bytes(ubuf.at[pl.ds(0, SIDE - 1)], u_send.at[1])
+    await_bytes(ubuf.at[pl.ds(0, SIDE - 1)], u_recv.at[1])
 
 
 def tile_kernel(
@@ -382,7 +384,7 @@
         leaves[part].start()
     load_state.wait()
     load_last.wait()
-    residual2 = state[0] - back_product(last[...], white_rt[...])
+    residual2 = state[0] - back_product(plane_sum(last[...]), white_rt[...])
     answer[...] = state[2] + state[1] * residual2
     leave_answer = pltpu.make_async_copy(answer, answer_out, out_sem.at[0])
     leave_answer.start()
@@ -401,13 +403,12 @@
             jax.ShapeDtypeStruct((WIDTH, EPOCHS), BF16),
             jax.ShapeDtypeStruct((EPOCHS, WIDTH), BF16),
             jax.ShapeDtypeStruct((3, 8, WIDTH), F32),
-            jax.ShapeDtypeStruct((16, EPOCHS), BF16),
+            jax.ShapeDtypeStruct((SIDE, 16, LANES), BF16),
         ),
         in_specs=[hbm, hbm, hbm, smem, smem],
         out_specs=(hbm, hbm, hbm, hbm),
         scratch_shapes=[
             pltpu.VMEM((3, 8, WIDTH), F32),
-            pltpu.VMEM((16, EPOCHS), BF16),
             pltpu.VMEM((BLOCK, WIDTH), BF16),
             pltpu.VMEM((1, EPOCHS), F32),
             pltpu.VMEM((8, WIDTH), F32),
@@ -419,7 +420,7 @@
             pltpu.VMEM((WIDTH, EPOCHS), BF16),
             pltpu.VMEM((EPOCHS, WIDTH), BF16),
             pltpu.VMEM((2, 16, LANES), BF16),
-            pltpu.VMEM((2, SIDE, 16, LANES), BF16),
+            pltpu.VMEM((SIDE, 16, LANES), BF16),
             pltpu.VMEM((SIDE, 16, LANES), BF16),
             pltpu.VMEM((CHUNKS, 16, LANES), BF16),
             dma((3,)), dma((4,)),
@@ -447,7 +448,7 @@
             pltpu.VMEM((WIDTH, EPOCHS), BF16),
             pltpu.VMEM((EPOCHS, WIDTH), BF16),
             pltpu.VMEM((3, 8, WIDTH), F32),
-            pltpu.VMEM((16, EPOCHS), BF16),
+            pltpu.VMEM((SIDE, 16, LANES), BF16),
             pltpu.VMEM((8, WIDTH), F32),
             pltpu.VMEM((STEPS, STEP, WIDTH), F32),
             dma((3 + STEPS,)), dma((1 + STEPS,)),

time: 44.6 us -> 44 us (0.987)
  Pallas kernels: 42.5 us -> 41.9 us
    pallas_call x1, Pallas kernels: 37.2 us -> 36.6 us  [body(): pl.pallas_call(kernel, out_shape=(jax.ShapeDtypeStruct((WIDTH, EPOCHS), B...]
where the time goes in v4:
time: 44 us; the launch traced here: 43.8 us
  Pallas kernels  41.9 us (95%)
  between operations  1.93 us (4%)
    pallas_call x1, Pallas kernels, body(): pl.pallas_call(kernel, out_shape=(jax.ShapeDtypeStruct((WIDTH, EPOCHS), B...  36.6 us
    pallas_call x1, Pallas kernels, body(): pl.pallas_call(tile_kernel, out_shape=(jax.ShapeDtypeStruct((WIDTH, WIDTH...  5.29 us

profile of v4, /device:TPU:1, one launch (start us, length us, event | category | flops | bytes accessed | tf_op | source)
XLA Modules:
  0.0 43.8 jit_solution(14887698535207034357)
XLA Ops:
  1.9 36.6 %gather_and_solve.1 = (bf16[1536,256]{1,0:T(8,128)(2,1)}, bf16[256,1536]{1,0:T(8,128)(2,1)}, f32[3,8,1536]{2,1,0:T(8,128)}, bf16[16,16,128]{2,1,0:T(8,128)(2,1)}) custom-call(bf16[16,1536]{1,0:T(8,128)(2,1)} %design_in.1, f32[1,256]{1,0:T(1,128)} %bitcast.4, f32[8,1536]{1,0:T(8,128)} %bitcast.3, f32[1]{0:T(128)S(6)} %copy.7.lower, f32[1]{0:T(128)S(6)} %copy.8.upper), custom_call_target="tpu_custom_call" | custom-call | tf_op jit(solution)/shard_map/gather_and_solve/pallas_call | solution.py:400
  38.6 5.3 %normal_tile.1 = (f32[1536,1536]{1,0:T(8,128)}, f32[8,1536]{1,0:T(8,128)}) custom-call(bf16[1536,256]{1,0:T(8,128)(2,1)} %get-tuple-element.8.rt_in, bf16[256,1536]{1,0:T(8,128)(2,1)} %get-tuple-element.9.c_in, f32[3,8,1536]{2,1,0:T(8,128)} %get-tuple-element.10.state_in, bf16[16,16,128]{2,1,0:T(8,128)(2,1)} %get-tuple-element.11.last_in), custom_call_target="tpu_custom_call" | custom-call | tf_op jit(solution)/shard_map/normal_tile/pallas_call | solution.py:439

commit v5 on v4

--- a/solution.py
+++ b/solution.py
@@ -21,8 +21,11 @@
 LAST = (((1,), (1,)), ((), ()))
 
 
-def owner_of(chunk):
-    return (chunk // 3) * 4 + chunk % 3
+ASIDE = (1, 3, 0)
+
+
+def owner_of(chunk, start):
+    return ((chunk // 2) % 2) * 8 + ((start + ASIDE[chunk // 4]) % 4) * 2 + chunk % 2
 
 
 PLANE = tuple(sorted(((a, b) for a in range(2) for b in range(8) if a or b), key=lambda p: -(2 * p[0] + min(p[1], 8 - p[1]))))
@@ -76,7 +79,7 @@
 def kernel(
     design_in, taps_in, probes_in, lower, upper,
     rt_out, c_out, state_out, last_out,
-    state, design, taps, probes,
+    state, jac, design, taps, probes,
     cbuf, rsub, psub, filt, filt_t, white_rt, white_c, usend, ubuf, rs_send, rs_buf,
     in_sem, out_sem, c_send, c_recv, s_send, s_recv, p_send, p_recv, rs_ssem, rs_rsem,
     g_send, g_fwd, g_recv, u_send, u_recv,
@@ -87,8 +90,10 @@
     sibling = (r, c + 1 - 2 * k)
     z_next, z_prev = (h * 8 + (z + 1) % 8, c), (h * 8 + (z + 7) % 8, c)
     partner = ((1 - h) * 8 + z, c)
-    is_owner = c % 4 != 3
-    mine = (c // 4) * 3 + c % 4
+    start = z // 2
+    aside = (x - start + 4) % 4
+    is_owner = aside != 2
+    mine = jnp.where(aside == 1, 0, jnp.where(aside == 3, 1, 2)) * 4 + l * 2 + k
     on_diagonal = r == c
 
     def in_plane(place):
@@ -105,12 +110,14 @@
         load.start()
 
     barrier = pltpu.get_barrier_semaphore()
-    for place in PLANE:
-        pl.semaphore_signal(barrier, inc=1, device_id=(in_plane(place), r), device_id_type=MESH)
-
-    @pl.when(jnp.logical_not(on_diagonal))
-    def _():
-        pl.semaphore_signal(barrier, inc=1, device_id=(r, r), device_id_type=MESH)
+    @pl.when(is_owner)
+    def _():
+        for place in PLANE:
+            pl.semaphore_signal(barrier, inc=1, device_id=(in_plane(place), r), device_id_type=MESH)
+
+        @pl.when(jnp.logical_not(on_diagonal))
+        def _():
+            pl.semaphore_signal(barrier, inc=1, device_id=(r, r), device_id_type=MESH)
 
     for place in PLANE:
         pl.semaphore_signal(barrier, inc=1, device_id=(in_plane(place), c), device_id_type=MESH)
@@ -145,10 +152,10 @@
 
     loads[0].wait()
     loads[2].wait()
-    pl.semaphore_wait(barrier, 15 + 15 + 15 + jnp.where(on_diagonal, 0, 1))
+    pl.semaphore_wait(barrier, 15 + 15 + CHUNKS - jnp.where(on_diagonal, 1, 0))
 
     for chunk in range(CHUNKS):
-        owner = owner_of(chunk)
+        owner = owner_of(chunk, x)
         copy = remote(
             design.at[:, pl.ds(chunk * LANES, LANES)], rsub.at[r], s_send, s_recv, (c, owner)
         )
@@ -188,7 +195,7 @@
     ship(3, r, at(2), design)
     ship(4, r, at(-2), design)
     for chunk in range(CHUNKS):
-        owner = owner_of(chunk)
+        owner = owner_of(chunk, start)
         copy = remote(
             probes.at[:, pl.ds(chunk * LANES, LANES)], psub.at[c], p_send, p_recv, (r, owner)
         )
@@ -275,14 +282,19 @@
 
     forwards = []
 
-    def chunk_copy(chunk):
-        rows = white_rt.at[pl.ds(chunk * LANES, LANES)]
-        return remote(rows, rows, g_fwd.at[chunk], g_recv.at[chunk], sibling)
-
-    for chunk in range(CHUNKS):
-        owner = owner_of(chunk)
-        relay = jnp.logical_and(c != owner, k == owner % 2)
-        copy = chunk_copy(chunk)
+    def rows_of(chunk):
+        return pl.ds(pl.multiple_of(chunk * LANES, LANES), LANES)
+
+    def chunk_copy(i, chunk):
+        rows = white_rt.at[rows_of(chunk)]
+        return remote(rows, rows, g_fwd.at[i], g_recv.at[chunk], sibling)
+
+    def take_jacobi(chunk):
+        jac[:, rows_of(chunk)] = squares_over_epochs(white_rt[rows_of(chunk), :])
+
+    for i in range(CHUNKS // 2):
+        relay = c != (i % 2) * 8 + ((start + ASIDE[i // 2]) % 4) * 2 + k
+        copy = chunk_copy(i, 2 * i + k)
         forwards.append((relay, copy))
 
         @pl.when(relay)
@@ -290,14 +302,15 @@
             copy.wait_recv()
             copy.start()
 
-    for chunk in range(CHUNKS):
-        @pl.when(k != owner_of(chunk) % 2)
-        def _():
-            chunk_copy(chunk).wait_recv()
+    for i in range(CHUNKS // 2):
+        take_jacobi(2 * i + k)
+    for i in range(CHUNKS // 2):
+        chunk_copy(i, 2 * i + 1 - k).wait_recv()
+        take_jacobi(2 * i + 1 - k)
 
     leave_rt = pltpu.make_async_copy(white_rt, rt_out, out_sem.at[0])
     leave_rt.start()
-    jacobi = squares_over_epochs(white_rt[...])
+    jacobi = jac[...]
     direction0 = probes[...] / jacobi / wide_row(center)
     await_bytes(ubuf.at[pl.ds(0, SIDE - 1)], u_recv.at[0])
     residual1 = probes[...] - back_product(plane_sum(ubuf[...]), white_rt[...])
@@ -409,6 +422,7 @@
         out_specs=(hbm, hbm, hbm, hbm),
         scratch_shapes=[
             pltpu.VMEM((3, 8, WIDTH), F32),
+            pltpu.VMEM((8, WIDTH), F32),
             pltpu.VMEM((BLOCK, WIDTH), BF16),
             pltpu.VMEM((1, EPOCHS), F32),
             pltpu.VMEM((8, WIDTH), F32),
@@ -428,7 +442,7 @@
             dma, dma,
             dma, dma,
             dma, dma,
-            dma, dma((CHUNKS,)), dma((CHUNKS,)),
+            dma, dma((CHUNKS // 2,)), dma((CHUNKS,)),
             dma((2,)), dma((2,)),
         ],
         compiler_params=pltpu.CompilerParams(

time: 44 us -> 44.3 us (level)
  no operation moved by 1% of the time
where the time goes in v5:
time: 44.3 us; the launch traced here: 44.1 us
  Pallas kernels  42.2 us (95%)
  between operations  1.93 us (4%)
    pallas_call x1, Pallas kernels, body(): pl.pallas_call(kernel, out_shape=(jax.ShapeDtypeStruct((WIDTH, EPOCHS), B...  36.9 us
    pallas_call x1, Pallas kernels, body(): pl.pallas_call(tile_kernel, out_shape=(jax.ShapeDtypeStruct((WIDTH, WIDTH...  5.29 us

profile of v5, /device:TPU:1, one launch (start us, length us, event | category | flops | bytes accessed | tf_op | source)
XLA Modules:
  0.0 44.1 jit_solution(11187140052305382170)
XLA Ops:
  1.9 36.9 %gather_and_solve.1 = (bf16[1536,256]{1,0:T(8,128)(2,1)}, bf16[256,1536]{1,0:T(8,128)(2,1)}, f32[3,8,1536]{2,1,0:T(8,128)}, bf16[16,16,128]{2,1,0:T(8,128)(2,1)}) custom-call(bf16[16,1536]{1,0:T(8,128)(2,1)} %design_in.1, f32[1,256]{1,0:T(1,128)} %bitcast.4, f32[8,1536]{1,0:T(8,128)} %bitcast.3, f32[1]{0:T(128)S(6)} %copy.7.lower, f32[1]{0:T(128)S(6)} %copy.8.upper), custom_call_target="tpu_custom_call" | custom-call | tf_op jit(solution)/shard_map/gather_and_solve/pallas_call | solution.py:413
  38.8 5.3 %normal_tile.1 = (f32[1536,1536]{1,0:T(8,128)}, f32[8,1536]{1,0:T(8,128)}) custom-call(bf16[1536,256]{1,0:T(8,128)(2,1)} %get-tuple-element.8.rt_in, bf16[256,1536]{1,0:T(8,128)(2,1)} %get-tuple-element.9.c_in, f32[3,8,1536]{2,1,0:T(8,128)} %get-tuple-element.10.state_in, bf16[16,16,128]{2,1,0:T(8,128)(2,1)} %get-tuple-element.11.last_in), custom_call_target="tpu_custom_call" | custom-call | tf_op jit(solution)/shard_map/normal_tile/pallas_call | solution.py:453

commit v6 on v5

--- a/solution.py
+++ b/solution.py
@@ -189,11 +189,11 @@
     def at(steps):
         return (h * 8 + (z + steps + 8) % 8, c)
 
-    ship(0, r, at(1), design)
-    ship(1, r, at(-1), design)
     ship(2, r, partner, design)
     ship(3, r, at(2), design)
     ship(4, r, at(-2), design)
+    ship(0, r, at(1), design)
+    ship(1, r, at(-1), design)
     for chunk in range(CHUNKS):
         owner = owner_of(chunk, start)
         copy = remote(
@@ -212,10 +212,10 @@
     cbuf[r] = design[...]
 
     await_block(block_of(True, 0))
+    ship(7, block_of(True, 0), at(2))
+    ship(8, block_of(True, 0), at(-2))
     ship(5, block_of(True, 0), at(1))
     ship(6, block_of(True, 0), at(-1))
-    ship(7, block_of(True, 0), at(2))
-    ship(8, block_of(True, 0), at(-2))
     my_rows = pl.ds(pl.multiple_of(mine * LANES, LANES), LANES)
 
     @pl.when(is_owner)
@@ -251,6 +251,25 @@
                 ).start()
         remote(white_rt.at[my_rows], white_rt.at[my_rows], g_send, g_recv.at[mine], sibling).start()
 
+    def exchange_start(turn, packed, slots):
+        usend[turn] = packed
+        for place in PLANE:
+            remote(
+                usend.at[turn], slots.at[r], u_send.at[turn], u_recv.at[turn], (in_plane(place), c)
+            ).start()
+
+    @pl.when(is_owner)
+    def _():
+        await_bytes(rs_buf.at[pl.ds(0, CHUNKS - 1)], rs_rsem)
+
+    @pl.when(jnp.logical_not(is_owner))
+    def _():
+        await_bytes(rs_buf, rs_rsem)
+
+    summed = jnp.sum(rs_buf[...].astype(F32), axis=0).astype(BF16)
+    exchange_start(0, summed, ubuf)
+    ubuf[r] = summed
+
     await_block(block_of(False, -2))
     ship(9, block_of(False, -2), at(1))
     await_block(block_of(False, 2))
@@ -261,25 +280,6 @@
     await_block(block_of(True, 2))
     ship(13, block_of(True, 2), at(-1))
     ship(14, block_of(True, 2 * way), at(-2 * way))
-    def exchange_start(turn, packed, slots):
-        usend[turn] = packed
-        for place in PLANE:
-            remote(
-                usend.at[turn], slots.at[r], u_send.at[turn], u_recv.at[turn], (in_plane(place), c)
-            ).start()
-
-    @pl.when(is_owner)
-    def _():
-        await_bytes(rs_buf.at[pl.ds(0, CHUNKS - 1)], rs_rsem)
-
-    @pl.when(jnp.logical_not(is_owner))
-    def _():
-        await_bytes(rs_buf, rs_rsem)
-
-    summed = jnp.sum(rs_buf[...].astype(F32), axis=0).astype(BF16)
-    exchange_start(0, summed, ubuf)
-    ubuf[r] = summed
-
     forwards = []
 
     def rows_of(chunk):

time: 44.3 us -> 44.1 us (level)
  no operation moved by 1% of the time
where the time goes in v6:
time: 44.1 us; the launch traced here: 43.9 us
  Pallas kernels  42 us (95%)
  between operations  1.93 us (4%)
    pallas_call x1, Pallas kernels, body(): pl.pallas_call(kernel, out_shape=(jax.ShapeDtypeStruct((WIDTH, EPOCHS), B...  36.7 us
    pallas_call x1, Pallas kernels, body(): pl.pallas_call(tile_kernel, out_shape=(jax.ShapeDtypeStruct((WIDTH, WIDTH...  5.29 us

profile of v6, /device:TPU:1, one launch (start us, length us, event | category | flops | bytes accessed | tf_op | source)
XLA Modules:
  0.0 43.9 jit_solution(15194690332635340394)
XLA Ops:
  1.9 36.7 %gather_and_solve.1 = (bf16[1536,256]{1,0:T(8,128)(2,1)}, bf16[256,1536]{1,0:T(8,128)(2,1)}, f32[3,8,1536]{2,1,0:T(8,128)}, bf16[16,16,128]{2,1,0:T(8,128)(2,1)}) custom-call(bf16[16,1536]{1,0:T(8,128)(2,1)} %design_in.1, f32[1,256]{1,0:T(1,128)} %bitcast.4, f32[8,1536]{1,0:T(8,128)} %bitcast.3, f32[1]{0:T(128)S(6)} %copy.7.lower, f32[1]{0:T(128)S(6)} %copy.8.upper), custom_call_target="tpu_custom_call" | custom-call | tf_op jit(solution)/shard_map/gather_and_solve/pallas_call | solution.py:413
  38.6 5.3 %normal_tile.1 = (f32[1536,1536]{1,0:T(8,128)}, f32[8,1536]{1,0:T(8,128)}) custom-call(bf16[1536,256]{1,0:T(8,128)(2,1)} %get-tuple-element.8.rt_in, bf16[256,1536]{1,0:T(8,128)(2,1)} %get-tuple-element.9.c_in, f32[3,8,1536]{2,1,0:T(8,128)} %get-tuple-element.10.state_in, bf16[16,16,128]{2,1,0:T(8,128)(2,1)} %get-tuple-element.11.last_in), custom_call_target="tpu_custom_call" | custom-call | tf_op jit(solution)/shard_map/normal_tile/pallas_call | solution.py:453
